TPU v7x, 32 devices: a whole 2x2x4 slice. The times are simulated.
32 devices in a mesh: tm: 4 (over y, x), space: 8 (over z, core).
Axes of the slice: x: 2, y: 2, z: 4, core: 2. Of those that a mesh axis runs over, the one named last changes fastest.
Arguments:
- spectrum: float32 [2, 512, 64, 1024], P(None, 'tm', 'space'), may hold values from -6 to 6
- diffusivity: float32 [64, 1024], P('space'), may hold values from 0.5 to 2
Outputs:
- solution: float32 [2, 512, 64, 1024], P(None, 'tm', 'space')
All inputs are finite; a program needn't handle non-finite values.
Results may differ from a plain program's by a relative error of at most 0.00016.
Values sent between devices are 32-bit elements; how exact they have to be, the bound alone decides.
A program may use at most 128 MiB of HBM per device.

v0:
```python
import math

import jax
import jax.numpy as jnp
import numpy as np
from jax import lax
from jax.sharding import PartitionSpec as P

alpha_wrap = 0.25
step_rate = 0.5
flow_speed = 2.0
sweep_weights = [
    1.0 / (1.0 + 0.7 * math.cos(math.pi * (2 * order + 1) / 6.0)) for order in range(3)
]


def extended_2(block, sides, width):
    for axis, dim in sides:
        count = lax.axis_size(axis)
        forward = [(i, i + 1) for i in range(count - 1)]
        backward = [(target, source) for source, target in forward]
        low = lax.ppermute(
            lax.slice_in_dim(block, block.shape[dim] - width, None, axis=dim), axis, forward
        )
        high = lax.ppermute(lax.slice_in_dim(block, 0, width, axis=dim), axis, backward)
        block = jnp.concatenate([low, block, high], axis=dim)
    return block


def reverse_bits(number, bit_count):
    result = number * 0
    for bit_place in range(bit_count):
        result = result + (number >> bit_place & 1) * (1 << bit_count - 1 - bit_place)
    return result


def shift_parts(freq_ids, total_steps):
    phase_angle = freq_ids.astype(jnp.float32) * (2.0 * math.pi / total_steps)
    root_scale = alpha_wrap ** (1.0 / total_steps)
    return (
        step_rate * (1.0 - root_scale * jnp.cos(phase_angle)),
        step_rate * root_scale * jnp.sin(phase_angle),
    )


def divide_diag(residual, diag_real, diag_imag, magnitude):
    real_part = (residual[0] * diag_real + residual[1] * diag_imag) / magnitude
    imag_part = (residual[1] * diag_real - residual[0] * diag_imag) / magnitude
    return jnp.stack([real_part, imag_part])


def apply_operator(current, diffusion, diag_real, diag_imag):
    padded = jnp.pad(current, ((0, 0), (0, 0), (0, 0), (1, 1)))
    center = padded[:, :, 1:-1, 1:-1]
    from_north = padded[:, :, :-2, 1:-1]
    from_south = padded[:, :, 2:, 1:-1]
    from_west = padded[:, :, 1:-1, :-2]
    from_east = padded[:, :, 1:-1, 2:]
    beside_all = from_north + from_south + from_west + from_east
    real_part = (
        diag_real * center[0]
        - diag_imag * center[1]
        - diffusion * beside_all[0]
        - flow_speed * from_north[0]
    )
    imag_part = (
        diag_real * center[1]
        + diag_imag * center[0]
        - diffusion * beside_all[1]
        - flow_speed * from_north[1]
    )
    return jnp.stack([real_part, imag_part])


def complex_scale(values, cos_part, sin_part):
    return jnp.stack(
        [cos_part * values[0] - sin_part * values[1], sin_part * values[0] + cos_part * values[1]]
    )


def on_device(spectrum, diffusivity):
    local_count = spectrum.shape[1]
    row_count = spectrum.shape[2]
    col_count = spectrum.shape[3]
    tm_count = lax.axis_size("tm")
    bit_count = tm_count.bit_length() - 1
    total_steps = local_count * tm_count
    tm_place = lax.axis_index("tm")
    residue = reverse_bits(tm_place, bit_count)
    index_f = jnp.arange(local_count, dtype=jnp.int32)
    freq_ids = index_f * tm_count + residue
    lam_real, lam_imag = shift_parts(freq_ids, total_steps)
    diag_real = lam_real[:, None, None] + 4.0 * diffusivity + flow_speed
    diag_imag = lam_imag[:, None, None] + jnp.zeros_like(diag_real)
    magnitude = diag_real * diag_real + diag_imag * diag_imag
    current = sweep_weights[0] * divide_diag(spectrum, diag_real, diag_imag, magnitude)
    for order in (1, 2):
        extended = extended_2(current, (("space", 2),), 1)
        applied = apply_operator(extended, diffusivity, diag_real, diag_imag)
        current = current + sweep_weights[order] * divide_diag(
            spectrum - applied, diag_real, diag_imag, magnitude
        )
    grid_angle = (index_f[:, None] * index_f[None, :] % local_count).astype(jnp.float32) * (
        2.0 * math.pi / local_count
    )
    cosine = jnp.cos(grid_angle)
    sine = jnp.sin(grid_angle)
    dft_table = jnp.concatenate(
        [jnp.concatenate([cosine, -sine], 1), jnp.concatenate([sine, cosine], 1)], 0
    )
    flat_field = current.reshape(2 * local_count, row_count * col_count)
    spectral = jnp.dot(dft_table, flat_field, precision=lax.Precision.HIGHEST).reshape(
        2, local_count, row_count, col_count
    )
    twist_angle = (residue * index_f % total_steps).astype(jnp.float32) * (
        2.0 * math.pi / total_steps
    )
    twisted = complex_scale(
        spectral, jnp.cos(twist_angle)[:, None, None], jnp.sin(twist_angle)[:, None, None]
    )
    outgoing = twisted.reshape(2, 1, local_count, row_count, col_count)
    arrived = lax.all_to_all(outgoing, "tm", split_axis=4, concat_axis=1, tiled=True)
    source_residue = np.array([reverse_bits(source, bit_count) for source in range(tm_count)])
    target_place = np.arange(tm_count)
    class_index = target_place[:, None] * source_residue[None, :] % tm_count
    class_angle = jnp.asarray(class_index, dtype=jnp.int32).astype(jnp.float32) * (
        2.0 * math.pi / tm_count
    )
    class_cos = jnp.cos(class_angle)
    class_sin = jnp.sin(class_angle)
    arrived_real = arrived[0].reshape(tm_count, -1)
    arrived_imag = arrived[1].reshape(tm_count, -1)
    high = lax.Precision.HIGHEST
    combined_real = jnp.dot(class_cos, arrived_real, precision=high) - jnp.dot(
        class_sin, arrived_imag, precision=high
    )
    combined_imag = jnp.dot(class_sin, arrived_real, precision=high) + jnp.dot(
        class_cos, arrived_imag, precision=high
    )
    combined = jnp.stack([combined_real, combined_imag]).reshape(arrived.shape)
    returned = lax.all_to_all(combined, "tm", split_axis=1, concat_axis=4, tiled=True)
    temporal = returned.reshape(2, local_count, row_count, col_count)
    step_ids = (tm_place * local_count + index_f).astype(jnp.float32)
    factor = jnp.exp(step_ids * (-math.log(alpha_wrap) / total_steps)) / math.sqrt(total_steps)
    return temporal * factor[None, :, None, None]


def solution(mesh):
    in_specs = (P(None, "tm", "space", None), P("space", None))
    out_specs = P(None, "tm", "space", None)
    return jax.shard_map(
        on_device, mesh=mesh, in_specs=in_specs, out_specs=out_specs, check_vma=False
    )
```

profile of v0, /device:TPU:9, one launch (start us, length us, event | category | flops | bytes accessed | tf_op | source)
XLA Modules:
  0.0 493.6 jit_solution(9691512998281421170)
XLA Ops:
  0.9 8.2 %copy.26 = f32[2,128,8,1024]{3,1,2,0:T(8,128)S(1)} copy(f32[2,128,8,1024]{3,2,1,0:T(8,128)} %param.3) | data formatting | bytes 16777216 | tf_op args[0]
  20.2 9.6 %collective-permute-done = f32[2,128,1,1024]{3,1,2,0:T(8,128)S(1)} collective-permute-done((f32[2,128,1,1024]{3,1,2,0:T(8,128)S(1)}, f32[2,128,1,1024]{3,1,2,0:T(8,128)S(1)}, u32[]{:S(2)}, u32[]{:S(2)}) %collective-permute-start) | collective-permute-done | bytes 1048608 | tf_op jit(solution)/shard_map/ppermute | solution.py:22
  35.2 8.0 %select_maximum_fusion.2 = f32[2,128,10,1026]{3,1,2,0:T(8,128)} fusion(f32[2,128,1,1024]{3,1,2,0:T(8,128)S(1)} %collective-permute-done.1, f32[2,128,8,1024]{3,1,2,0:T(8,128)S(1)} %maximum_multiply_fusion, f32[2,128,1,1024]{3,1,2,0:T(8,128)S(1)} %collective-permute-done), kind=kLoop, calls=%fused_computation.10 | loop fusion | flops 21012480 | bytes 20992000 | tf_op jit(solution)/shard_map/concatenate | solution.py:26
  43.1 11.1 %fusion.8 = f32[2,128,8,1024]{3,1,2,0:T(8,128)} fusion(f32[2,128,8,1024]{3,1,2,0:T(8,128)S(1)} %maximum_multiply_fusion, f32[2,128,1,1024]{3,1,2,0:T(8,128)} %copy-done.10, f32[2,128,10,1026]{3,1,2,0:T(8,128)} %select_maximum_fusion.2, f32[2,128,1,1024]{3,1,2,0:T(8,128)} %copy-done.12), kind=kLoop, calls=%fused_computation.24 | loop fusion | flops 10485760 | bytes 35651584 | tf_op jit(solution)/shard_map/add | solution.py:59
  54.3 7.7 %fusion.15 = (f32[1,128,8,1024]{3,1,2,0:T(8,128)S(1)}, f32[1,128,8,1024]{3,1,2,0:T(8,128)}) fusion(f32[2,128,8,1024]{3,1,2,0:T(8,128)S(1)} %maximum_multiply_fusion, f32[2,128,1,1024]{3,1,2,0:T(8,128)} %copy-done.10, f32[2,128,8,1024]{3,1,2,0:T(8,128)} %fusion.8, f32[8,1024]{1,0:T(8,128)S(1)} %copy-done.13, f32[128]{0:T(128)S(1)} %get-tuple-element.25, ...), kind=kLoop, calls=%fused_computation.41 | loop fusion | flops 18874368 | bytes 34669568 | tf_op jit(solution)/shard_map/sub | solution.py:61
  62.0 9.4 %maximum_subtract_fusion = f32[2,128,8,1024]{3,1,2,0:T(8,128)S(1)} fusion(f32[1,128,8,1024]{3,1,2,0:T(8,128)} %get-tuple-element.8, f32[1,128,8,1024]{3,1,2,0:T(8,128)S(1)} %get-tuple-element.7, f32[2,128,8,1024]{3,2,1,0:T(8,128)} %param.3), kind=kLoop, calls=%fused_computation.28 | loop fusion | flops 4194304 | bytes 25165824 | tf_op jit(solution)/shard_map/sub | solution.py:101
  82.2 8.2 %collective-permute-done.2 = f32[2,128,1,1024]{3,1,2,0:T(8,128)S(1)} collective-permute-done((f32[2,128,1,1024]{3,1,2,0:T(8,128)S(1)}, f32[2,128,1,1024]{3,1,2,0:T(8,128)S(1)}, u32[]{:S(2)}, u32[]{:S(2)}) %collective-permute-start.2) | collective-permute-done | bytes 1048608 | tf_op jit(solution)/shard_map/ppermute | solution.py:22
  95.8 8.0 %select_maximum_fusion = f32[2,128,10,1026]{3,1,2,0:T(8,128)} fusion(f32[2,128,1,1024]{3,1,2,0:T(8,128)S(1)} %collective-permute-done.3, f32[2,128,8,1024]{3,1,2,0:T(8,128)S(1)} %maximum_add_fusion, f32[2,128,1,1024]{3,1,2,0:T(8,128)S(1)} %collective-permute-done.2), kind=kLoop, calls=%fused_computation.8 | loop fusion | flops 21012480 | bytes 20992000 | tf_op jit(solution)/shard_map/concatenate | solution.py:26
  103.7 11.4 %fusion.4 = f32[2,128,8,1024]{3,1,2,0:T(8,128)} fusion(f32[2,128,8,1024]{3,1,2,0:T(8,128)S(1)} %maximum_add_fusion, f32[2,128,1,1024]{3,1,2,0:T(8,128)} %copy-done.9, f32[2,128,10,1026]{3,1,2,0:T(8,128)} %select_maximum_fusion, f32[2,128,1,1024]{3,1,2,0:T(8,128)} %copy-done.11), kind=kLoop, calls=%fused_computation.20 | loop fusion | flops 10485760 | bytes 35651584 | tf_op jit(solution)/shard_map/add | solution.py:59
  115.1 7.7 %fusion.12 = (f32[1,128,8,1024]{3,1,2,0:T(8,128)S(1)}, f32[1,128,8,1024]{3,1,2,0:T(8,128)}) fusion(f32[2,128,8,1024]{3,1,2,0:T(8,128)S(1)} %maximum_add_fusion, f32[2,128,1,1024]{3,1,2,0:T(8,128)} %copy-done.9, f32[2,128,8,1024]{3,1,2,0:T(8,128)} %fusion.4, f32[8,1024]{1,0:T(8,128)S(1)} %copy-done.13, f32[128]{0:T(128)S(1)} %get-tuple-element.25, ...), kind=kLoop, calls=%fused_computation.38 | loop fusion | flops 18874368 | bytes 34669568 | tf_op jit(solution)/shard_map/sub | solution.py:61
  122.8 9.4 %maximum_subtract_fusion.1 = f32[2,128,8,1024]{3,1,2,0:T(8,128)S(1)} fusion(f32[1,128,8,1024]{3,1,2,0:T(8,128)} %get-tuple-element.6, f32[1,128,8,1024]{3,1,2,0:T(8,128)S(1)} %get-tuple-element.5, f32[2,128,8,1024]{3,2,1,0:T(8,128)} %param.3), kind=kLoop, calls=%fused_computation.30 | loop fusion | flops 4194304 | bytes 25165824 | tf_op jit(solution)/shard_map/sub | solution.py:101
  145.2 8.2 %copy.30 = f32[2,128,8,1024]{3,2,1,0:T(8,128)S(1)} copy(f32[2,128,8,1024]{3,1,2,0:T(8,128)} %fusion.9) | data formatting | bytes 16777216 | tf_op jit(solution)/shard_map/add | solution.py:100
  153.5 8.8 %copy.42 = f32[32,8,8,1024]{3,1,2,0:T(8,128)S(1)} copy(f32[32,8,8,1024]{3,2,1,0:T(8,128)S(1)} %bitcast.55) | data formatting | bytes 16777216
  162.3 8.3 %fusion.25 = f32[256,8192]{1,0:T(8,128)S(1)} fusion(f32[256,8192]{1,0:T(8,128)S(1)} %bitcast.53, f32[128,128]{1,0:T(8,128)S(1)} %get-tuple-element.30, f32[128,128]{1,0:T(8,128)S(1)} %get-tuple-element.29, f32[128,128]{1,0:T(8,128)S(1)} %fusion.41), kind=kOutput, calls=%fused_computation.68 | convolution fusion | flops 6442647552 | bytes 16973824 | tf_op jit(solution)/shard_map/dot_general | solution.py:112
  184.2 7.8 %copy.44 = f32[16,8,8,1024]{3,2,1,0:T(8,128)} copy(f32[16,8,8,1024]{3,1,2,0:T(8,128)} %bitcast.61) | data formatting | bytes 8388608
  202.3 95.7 %all_to_all.30 = f32[2,1,128,8,1024]{2,3,0,1,4:T(8,128)S(1)} all-to-all(f32[2,1,128,8,1024]{2,3,0,1,4:T(8,128)S(1)} %maximum_bitcast_fusion), channel_id=1, replica_groups=mesh['tm'=4,'space'=8] {'tm'}, dimensions={4} | all-to-all | bytes 16777216 | tf_op jit(solution)/shard_map/all_to_all | solution.py:122
  328.2 9.6 %fusion.53 = f32[4,262144]{1,0:T(4,128)S(1)} fusion(f32[4,4]{1,0:T(4,128)S(1)} %copy-done.14, f32[4,262144]{1,0:T(4,128)} %reshape_squeeze.6), kind=kOutput, calls=%fused_computation.107 | convolution fusion | flops 50331648 | bytes 8388672 | tf_op jit(solution)/shard_map/dot_general | solution.py:134
  337.9 7.6 %fusion.54 = f32[4,262144]{1,0:T(4,128)S(1)} fusion(f32[4,4]{1,0:T(4,128)S(1)} %copy-done.15, f32[4,262144]{1,0:T(4,128)S(1)} %copy-done.4), kind=kOutput, calls=%fused_computation.108 | convolution fusion | flops 50331648 | bytes 8388672 | tf_op jit(solution)/shard_map/dot_general | solution.py:137
  345.5 8.8 %convolution_subtract_fusion = f32[4,262144]{1,0:T(4,128)S(1)} fusion(f32[4,262144]{1,0:T(4,128)S(1)} %fusion.53, f32[4,4]{1,0:T(4,128)S(1)} %copy-done.15, f32[4,262144]{1,0:T(4,128)S(1)} %copy-done), kind=kOutput, calls=%fused_computation.1 | convolution fusion | flops 51380224 | bytes 12582976 | tf_op jit(solution)/shard_map/dot_general | solution.py:134
  355.2 8.6 %convolution_add_fusion = f32[4,262144]{1,0:T(4,128)S(1)} fusion(f32[4,262144]{1,0:T(4,128)S(1)} %fusion.54, f32[4,4]{1,0:T(4,128)S(1)} %copy-done.14, f32[4,262144]{1,0:T(4,128)S(1)} %copy-done), kind=kOutput, calls=%fused_computation | convolution fusion | flops 51380224 | bytes 12582976 | tf_op jit(solution)/shard_map/dot_general | solution.py:137
  374.3 92.6 %all-to-all-done.1 = f32[2,4,128,8,256]{4,3,2,0,1:T(8,128)} async-done(((f32[2,4,128,8,256]{4,3,2,0,1:T(8,128)}), f32[2,4,128,8,256]{4,3,2,0,1:T(8,128)}, u32[]{:S(2)}, u32[]{:S(2)}) %all-to-all-start.1) | async-done | bytes 8388640 | tf_op jit(solution)/shard_map/all_to_all | solution.py:141
  466.9 10.0 %copy.40 = f32[2,4,128,8,256]{2,4,1,3,0:T(8,128)} copy(f32[2,4,128,8,256]{4,3,2,0,1:T(8,128)} %all-to-all-done.1) | data formatting | bytes 16777216 | tf_op jit(solution)/shard_map/all_to_all | solution.py:141
  476.9 7.4 %bitcast_multiply_fusion = f32[2,128,8,1024]{1,3,2,0:T(8,128)} fusion(f32[2,4,128,8,256]{2,4,1,3,0:T(8,128)} %copy.40, f32[128]{0:T(128)S(1)} %exponential_multiply_fusion), kind=kLoop, calls=%fused_computation.35 | loop fusion | flops 2097152 | bytes 16777728 | tf_op jit(solution)/shard_map/mul | solution.py:145
  484.4 8.8 %copy.41 = f32[2,128,8,1024]{3,2,1,0:T(8,128)} copy(f32[2,128,8,1024]{1,3,2,0:T(8,128)} %bitcast_multiply_fusion) | data formatting | bytes 16777216 | tf_op jit(solution)/shard_map/mul | solution.py:145
  (69 shorter events, 111.8 us)
Async XLA Ops:
  11.2 3.0 copy-start.1
  14.3 15.5 %collective-permute-start = (f32[2,128,1,1024]{3,1,2,0:T(8,128)S(1)}, f32[2,128,1,1024]{3,1,2,0:T(8,128)S(1)}, u32[]{:S(2)}, u32[]{:S(2)}) collective-permute-start(f32[2,128,1,1024]{3,1,2,0:T(8,128)S(1)} %get-tuple-element.24), channel_id=1, source_target_pairs={{0,1},{1,2},{2,3},{3,4},{4,5},{5,6},{6,7},{8,9},{9,10},{10,11},{11... | collective-permute-start | bytes 3145736 | tf_op jit(solution)/shard_map/ppermute | solution.py:22
  18.0 16.1 %collective-permute-start.1 = (f32[2,128,1,1024]{3,1,2,0:T(8,128)S(1)}, f32[2,128,1,1024]{3,1,2,0:T(8,128)S(1)}, u32[]{:S(2)}, u32[]{:S(2)}) collective-permute-start(f32[2,128,1,1024]{3,1,2,0:T(8,128)S(1)} %get-tuple-element.23), channel_id=1, source_target_pairs={{1,0},{2,1},{3,2},{4,3},{5,4},{6,5},{7,6},{9,8},{10,9},{11,10},{12... | collective-permute-start | bytes 3145736 | tf_op jit(solution)/shard_map/ppermute | solution.py:25
  29.8 4.4 copy-start.10
  34.2 1.0 copy-start.12
  43.1 11.1 %copy-start.13 = (f32[8,1024]{1,0:T(8,128)S(1)}, f32[8,1024]{1,0:T(8,128)}, u32[]{:S(2)}) copy-start(f32[8,1024]{1,0:T(8,128)} %param.4) | copy-start | bytes 98308
  71.3 2.2 copy-start.2
  73.4 2.1 copy-start.5
  73.4 3.2 copy-start.7
  76.8 13.7 %collective-permute-start.2 = (f32[2,128,1,1024]{3,1,2,0:T(8,128)S(1)}, f32[2,128,1,1024]{3,1,2,0:T(8,128)S(1)}, u32[]{:S(2)}, u32[]{:S(2)}) collective-permute-start(f32[2,128,1,1024]{3,1,2,0:T(8,128)S(1)} %get-tuple-element.22), channel_id=1, source_target_pairs={{0,1},{1,2},{2,3},{3,4},{4,5},{5,6},{6,7},{8,9},{9,10},{10,11},{11... | collective-permute-start | bytes 3145736 | tf_op jit(solution)/shard_map/ppermute | solution.py:22
  78.7 16.1 %collective-permute-start.3 = (f32[2,128,1,1024]{3,1,2,0:T(8,128)S(1)}, f32[2,128,1,1024]{3,1,2,0:T(8,128)S(1)}, u32[]{:S(2)}, u32[]{:S(2)}) collective-permute-start(f32[2,128,1,1024]{3,1,2,0:T(8,128)S(1)} %get-tuple-element.21), channel_id=1, source_target_pairs={{1,0},{2,1},{3,2},{4,3},{5,4},{6,5},{7,6},{9,8},{10,9},{11,10},{12... | collective-permute-start | bytes 3145736 | tf_op jit(solution)/shard_map/ppermute | solution.py:25
  90.4 4.4 copy-start.9
  94.8 1.0 copy-start.11
  132.2 3.5 copy-start.3
  132.2 5.0 %copy-start.6 = (f32[1,128,8,1024]{3,1,2,0:T(8,128)S(1)}, f32[1,128,8,1024]{3,1,2,0:T(8,128)}, u32[]{:S(2)}) copy-start(f32[1,128,8,1024]{3,1,2,0:T(8,128)} %copy-done.5) | copy-start | bytes 12582916
  132.2 6.2 %copy-start.8 = (f32[1,128,8,1024]{3,1,2,0:T(8,128)S(1)}, f32[1,128,8,1024]{3,1,2,0:T(8,128)}, u32[]{:S(2)}) copy-start(f32[1,128,8,1024]{3,1,2,0:T(8,128)} %copy-done.7) | copy-start | bytes 12582916
  321.9 6.3 %copy-start.14 = (f32[4,4]{1,0:T(4,128)S(1)}, f32[4,4]{1,0:T(4,128)}, u32[]{:S(2)}) copy-start(f32[4,4]{1,0:T(4,128)} %constant.79) | copy-start | bytes 196
  328.2 9.6 %copy-start.4 = (f32[4,262144]{1,0:T(4,128)S(1)}, f32[4,262144]{1,0:T(4,128)}, u32[]{:S(2)}) copy-start(f32[4,262144]{1,0:T(4,128)} %reshape_squeeze.6) | copy-start | bytes 12582916
  328.2 9.6 %copy-start.15 = (f32[4,4]{1,0:T(4,128)S(1)}, f32[4,4]{1,0:T(4,128)}, u32[]{:S(2)}) copy-start(f32[4,4]{1,0:T(4,128)} %constant.80) | copy-start | bytes 196
  337.9 7.7 %copy-start = (f32[4,262144]{1,0:T(4,128)S(1)}, f32[4,262144]{1,0:T(4,128)}, u32[]{:S(2)}) copy-start(f32[4,262144]{1,0:T(4,128)} %reshape_squeeze.7) | copy-start | bytes 12582916
  368.6 98.3 %all-to-all-start.1 = ((f32[2,4,128,8,256]{4,3,2,0,1:T(8,128)}), f32[2,4,128,8,256]{4,3,2,0,1:T(8,128)}, u32[]{:S(2)}, u32[]{:S(2)}) async-start(f32[2,4,128,8,256]{4,3,2,0,1:T(8,128)} %pad_maximum_fusion.2), calls=%async_computation.1 | async-start | bytes 16777216 | tf_op jit(solution)/shard_map/all_to_all | solution.py:141
where the time goes:
time: 501 us; the launch traced here: 494 us
  waiting for transfers between devices  119 us (24%)
  local copies, waits for them, and re-layouts  110 us (22%)
  other arithmetic  108 us (22%)
  blocking collectives  95.7 us (19%)
  matrix products  43 us (9%)
  starting transfers between devices  16.3 us (3%)
    all_to_all x1, blocking collectives, on_device(): lax.all_to_all(outgoing, 'tm', split_axis=4, concat_axis=1, tiled=True)  95.7 us
    all_to_all x1, waiting for transfers between devices, on_device(): lax.all_to_all(combined, 'tm', split_axis=1, concat_axis=4, tiled=True)  92.6 us
    unnamed x38, local copies, waits for them, and re-layouts  39.3 us
    add x2, other arithmetic, apply_operator(): beside_all = from_north + from_south + from_west + from_east  22.5 us
    sub x2, other arithmetic, on_device(): spectrum - applied  18.7 us
    ppermute x2, waiting for transfers between devices, extended_2(): lax.ppermute(lax.slice_in_dim(block, block.shape[dim] - width, None, axis...  17.8 us
    concatenate x2, other arithmetic, extended_2(): block = jnp.concatenate([low, block, high], axis=dim)  15.9 us
    sub x2, other arithmetic, apply_operator(): diag_real * center[0] - diag_imag * center[1] - diffusion * beside_all[0]  15.4 us
  transfers between devices with their start and end apart: 5, of which 5 were waited for; matrix products, arithmetic and copies ran while one was open for 0% of the time, Pallas kernels for 0%

commit v1 on v0

v1 whole, which is shorter than its diff:
```python
import functools
import math

import jax
import jax.numpy as jnp
import numpy as np
from jax import lax
from jax.experimental import pallas as pl
from jax.experimental.pallas import tpu as pltpu
from jax.sharding import PartitionSpec as P

alpha_wrap = 0.25
step_rate = 0.5
flow_speed = 2.0
sweep_weights = [
    1.0 / (1.0 + 0.7 * math.cos(math.pi * (2 * order + 1) / 6.0)) for order in range(3)
]
MESH = pl.DeviceIdType.MESH
HALO = 2


def reverse_bits(number, bit_count):
    result = number * 0
    for bit_place in range(bit_count):
        result = result + (number >> bit_place & 1) * (1 << bit_count - 1 - bit_place)
    return result


def make_tables(tm_count, local_count):
    bit_count = tm_count.bit_length() - 1
    total = tm_count * local_count
    place = np.arange(local_count)
    dft = np.zeros((tm_count, 2 * local_count, 2 * local_count))
    shifts = np.zeros((tm_count, 2 * local_count, 128))
    factors = np.zeros((tm_count, bit_count, 4))
    root_scale = alpha_wrap ** (1.0 / total)
    for dev in range(tm_count):
        residue = reverse_bits(dev, bit_count)
        freq = place * tm_count + residue
        phase = 2.0 * np.pi * (place[:, None] * freq[None, :] % total) / total
        grown = alpha_wrap ** (-place / total)[:, None] / math.sqrt(total)
        cosine, sine = grown * np.cos(phase), grown * np.sin(phase)
        dft[dev] = np.block([[cosine, -sine], [sine, cosine]])
        angle = 2.0 * np.pi * freq / total
        shifts[dev, :local_count] = (step_rate * (1.0 - root_scale * np.cos(angle)))[:, None]
        shifts[dev, local_count:] = (step_rate * root_scale * np.sin(angle))[:, None]
        for stage in range(bit_count):
            turn = (dev % (2 << stage)) / (2 << stage)
            unit, spun = (1.0, 0.0), (math.cos(2 * math.pi * turn), math.sin(2 * math.pi * turn))
            mine, theirs = (spun, unit) if dev >> stage & 1 else (unit, spun)
            scale = alpha_wrap ** (-dev / tm_count) if stage == bit_count - 1 else 1.0
            factors[dev, stage] = scale * np.array([*mine, *theirs])
    return (
        dft.astype(np.float32),
        shifts.astype(np.float32),
        factors.reshape(-1).astype(np.float32),
    )


def kernel(
    cfg, field, diffusion, dft_all, shift_all, factors, out,
    hold, mid, last, moved, grid_d, dft, shift,
    load_sem, table_sem, edge_send, edge_recv, move_send, move_recv, out_sem,
):
    stages, tm_count, count, rows, cols, parts, tile = cfg
    width = cols // parts
    d = lax.axis_index("tm")
    s = lax.axis_index("space")
    s_count = lax.axis_size("space")
    is_first, is_last = s == 0, s == s_count - 1
    not_first, not_last = s > 0, s < s_count - 1
    partners = [d + (1 << g) - (2 << g) * ((d // (1 << g)) % 2) for g in range(stages)]

    barrier = pltpu.get_barrier_semaphore()
    for partner in partners:
        pl.semaphore_signal(barrier, inc=1, device_id={"tm": partner}, device_id_type=MESH)

    @pl.when(not_first)
    def _():
        pl.semaphore_signal(barrier, inc=1, device_id={"space": s - 1}, device_id_type=MESH)

    @pl.when(not_last)
    def _():
        pl.semaphore_signal(barrier, inc=1, device_id={"space": s + 1}, device_id_type=MESH)

    row_order = [(turn + HALO) % rows for turn in range(rows)]
    loads = {
        row: pltpu.make_async_copy(field.at[row], hold.at[row + HALO], load_sem.at[row])
        for row in range(rows)
    }
    tables = [
        pltpu.make_async_copy(diffusion, grid_d.at[pl.ds(8, rows)], table_sem.at[0]),
        pltpu.make_async_copy(shift_all.at[d], shift, table_sem.at[1]),
        pltpu.make_async_copy(dft_all.at[d], dft, table_sem.at[2]),
    ]
    tables[0].start()
    tables[1].start()
    for row in range(rows):
        loads[row].start()
    tables[2].start()

    to_north = [
        pltpu.make_async_remote_copy(
            field.at[pl.ds(0, HALO)], hold.at[pl.ds(rows + HALO, HALO)],
            edge_send.at[0], edge_recv.at[0], device_id={"space": s - 1}, device_id_type=MESH),
        pltpu.make_async_remote_copy(
            diffusion, grid_d.at[pl.ds(8 + rows, rows)],
            edge_send.at[1], edge_recv.at[1], device_id={"space": s - 1}, device_id_type=MESH),
    ]
    to_south = [
        pltpu.make_async_remote_copy(
            field.at[pl.ds(rows - HALO, HALO)], hold.at[pl.ds(0, HALO)],
            edge_send.at[2], edge_recv.at[2], device_id={"space": s + 1}, device_id_type=MESH),
        pltpu.make_async_remote_copy(
            diffusion, grid_d.at[pl.ds(8 - rows, rows)],
            edge_send.at[3], edge_recv.at[3], device_id={"space": s + 1}, device_id_type=MESH),
    ]

    beside = lax.div(s + s_count - 1, s_count) + lax.div(2 * (s_count - 1) - s, s_count)
    pl.semaphore_wait(barrier, stages + beside)

    @pl.when(not_first)
    def _():
        for copy in to_north:
            copy.start()

    @pl.when(not_last)
    def _():
        for copy in to_south:
            copy.start()

    tables[0].wait()
    tables[1].wait()

    lanes = lax.broadcasted_iota(jnp.int32, (8, cols), 1)

    def each_block(body):
        def step(index, carry):
            low = pl.multiple_of(index * 8, 8)
            body(pl.ds(low, 8), pl.ds(pl.multiple_of(low + count, 8), 8))
            return carry

        lax.fori_loop(0, count // 8, step, 0)

    def inverse_diag(row, re, im):
        wide = jnp.concatenate
        local = jnp.broadcast_to(grid_d[pl.ds(8 + row, 1), :], (8, cols))
        diag_real = wide([shift[re, :]] * (cols // 128), axis=1) + (4.0 * local + flow_speed)
        diag_imag = wide([shift[im, :]] * (cols // 128), axis=1)
        scale = 1.0 / (diag_real * diag_real + diag_imag * diag_imag)
        return local, diag_real * scale, diag_imag * scale

    def over(real, imag, g_real, g_imag):
        return real * g_real + imag * g_imag, imag * g_real - real * g_imag

    def pull(ref, at, block, local):
        here = ref[at, block, :]
        west = jnp.where(lanes == 0, 0.0, pltpu.roll(here, 1, 1))
        east = jnp.where(lanes == cols - 1, 0.0, pltpu.roll(here, cols - 1, 1))
        north = ref[at - 1, block, :]
        south = ref[at + 1, block, :]
        return here, local * (north + south + west + east) + flow_speed * north

    w0, w1, w2 = sweep_weights

    def first_sweep(row):
        at = row + HALO

        def body(re, im):
            _, g_real, g_imag = inverse_diag(row, re, im)
            real, imag = over(hold[at, re, :], hold[at, im, :], g_real, g_imag)
            hold[at, re, :] = w0 * real
            hold[at, im, :] = w0 * imag

        each_block(body)

    def second_sweep(row):
        at = row + HALO
        keep = 1.0 - w1 + w1 / w0

        def body(re, im):
            local, g_real, g_imag = inverse_diag(row, re, im)
            here_real, pull_real = pull(hold, at, re, local)
            here_imag, pull_imag = pull(hold, at, im, local)
            real, imag = over(pull_real, pull_imag, g_real, g_imag)
            mid[row + 1, re, :] = keep * here_real + w1 * real
            mid[row + 1, im, :] = keep * here_imag + w1 * imag

        each_block(body)

    def third_sweep(row):
        def body(re, im):
            local, g_real, g_imag = inverse_diag(row, re, im)
            here_real, pull_real = pull(mid, row + 1, re, local)
            here_imag, pull_imag = pull(mid, row + 1, im, local)
            real, imag = over(pull_real, pull_imag, g_real, g_imag)
            at = row + HALO
            last[re, :] = (1.0 - w2) * here_real + (w2 / w0) * hold[at, re, :] + w2 * real
            last[im, :] = (1.0 - w2) * here_imag + (w2 / w0) * hold[at, im, :] + w2 * imag

        each_block(body)

    def columns(part):
        return pl.ds(pl.multiple_of(part * width, 128), width)

    def holder(stage, row):
        return hold.at[row + HALO] if stage == 0 else moved.at[stage - 1, row]

    def exchange(stage, row, part):
        cut = columns(part)
        return pltpu.make_async_remote_copy(
            holder(stage, row).at[:, cut], moved.at[stage, row, :, cut],
            move_send.at[stage, row, part], move_recv.at[stage, row, part],
            device_id={"tm": partners[stage]}, device_id_type=MESH)

    def write_out(row, part):
        cut = columns(part)
        return pltpu.make_async_copy(
            moved.at[stages - 1, row, :, cut], out.at[row, :, cut], out_sem.at[row, part])

    def place(chunk):
        return (chunk // parts + HALO) % rows, chunk % parts

    def combine(stage, chunk):
        row, part = place(chunk)
        exchange(stage, row, part).wait()
        cut = columns(part)
        mine, theirs = holder(stage, row), moved.at[stage, row]
        base = (d * stages + stage) * 4
        mr, mi, tr, ti = [factors[base + i] for i in range(4)]

        def body(re, im):
            a_real, a_imag = mine[re, cut], mine[im, cut]
            b_real, b_imag = theirs[re, cut], theirs[im, cut]
            theirs[re, cut] = mr * a_real - mi * a_imag + (tr * b_real - ti * b_imag)
            theirs[im, cut] = mr * a_imag + mi * a_real + (tr * b_imag + ti * b_real)

        each_block(body)
        if stage + 1 < stages:
            exchange(stage + 1, row, part).start()
        else:
            write_out(row, part).start()

    done_first, done_second = set(), set()

    def north_edge():
        @pl.when(not_first)
        def _():
            for copy in to_south:
                copy.wait_recv()
            for row in range(-HALO, 0):
                first_sweep(row)

        @pl.when(is_first)
        def _():
            hold[1] = jnp.zeros((2 * count, cols), jnp.float32)
            mid[0] = jnp.zeros((2 * count, cols), jnp.float32)

        need_first(0)

        @pl.when(not_first)
        def _():
            second_sweep(-1)

    def south_edge():
        @pl.when(not_last)
        def _():
            for copy in to_north:
                copy.wait_recv()
            for row in range(rows, rows + HALO):
                first_sweep(row)

        @pl.when(is_last)
        def _():
            hold[rows + HALO] = jnp.zeros((2 * count, cols), jnp.float32)
            mid[rows + 1] = jnp.zeros((2 * count, cols), jnp.float32)

        need_first(rows - 1)

        @pl.when(not_last)
        def _():
            second_sweep(rows)

    edges = {-1: north_edge, rows: south_edge}

    def need_first(row):
        if row in edges:
            if edges[row] is not None:
                run, edges[row] = edges[row], None
                run()
        elif row not in done_first:
            done_first.add(row)
            loads[row].wait()
            first_sweep(row)

    def need_second(row):
        if row in edges:
            need_first(row)
        elif row not in done_second:
            done_second.add(row)
            for near in (row - 1, row, row + 1):
                need_first(near)
            second_sweep(row)

    def solve_row(row, first):
        for near in (row - 1, row, row + 1):
            need_second(near)
        third_sweep(row)
        if first:
            tables[2].wait()
        for part in range(parts):
            def step(index, carry, part=part):
                cut = pl.ds(pl.multiple_of(part * width + index * tile, 128), tile)
                hold[row + HALO, :, cut] = jnp.dot(
                    dft[...], last[:, cut], precision=lax.Precision.HIGHEST,
                    preferred_element_type=jnp.float32)
                return carry

            lax.fori_loop(0, width // tile, step, 0)
            exchange(0, row, part).start()

    chunks = rows * parts
    lags = [1 + 2 * stage for stage in range(stages)]
    uniform = range(max(rows, lags[-1]), chunks + 1)

    def tick(now, checked):
        for stage in range(stages):
            if not checked or 0 <= now - lags[stage] < chunks:
                combine(stage, now - lags[stage])

    for now in range(uniform.start):
        if now < rows:
            solve_row(row_order[now], now == 0)
        tick(now, True)

    def steady(now, carry):
        tick(now, False)
        return carry

    lax.fori_loop(uniform.start, uniform.stop, steady, 0)
    for now in range(uniform.stop, chunks + lags[-1]):
        tick(now, True)

    def finish(chunk, carry):
        row, part = place(chunk)
        write_out(row, part).wait()
        return carry

    lax.fori_loop(0, chunks, finish, 0)

    @pl.when(not_first)
    def _():
        for copy in to_north:
            copy.wait_send()

    @pl.when(not_last)
    def _():
        for copy in to_south:
            copy.wait_send()


def on_device(spectrum, diffusivity):
    count, rows, cols = spectrum.shape[1:]
    tm_count = lax.axis_size("tm")
    stages = tm_count.bit_length() - 1
    parts, tile = 2, 256
    field = spectrum.transpose(2, 0, 1, 3).reshape(rows, 2 * count, cols)
    dft, shifts, factors = make_tables(tm_count, count)
    cfg = (stages, tm_count, count, rows, cols, parts, tile)
    high = 2 * count
    anywhere = pl.BlockSpec(memory_space=pl.ANY)
    f32 = jnp.float32
    result = pl.pallas_call(
        functools.partial(kernel, cfg),
        out_shape=jax.ShapeDtypeStruct((rows, high, cols), f32),
        in_specs=[anywhere] * 4 + [pl.BlockSpec(memory_space=pltpu.SMEM)],
        out_specs=anywhere,
        scratch_shapes=[
            pltpu.VMEM((rows + 2 * HALO, high, cols), f32),
            pltpu.VMEM((rows + 2, high, cols), f32),
            pltpu.VMEM((high, cols), f32),
            pltpu.VMEM((stages, rows, high, cols), f32),
            pltpu.VMEM((8 + 2 * rows, cols), f32),
            pltpu.VMEM((high, high), f32),
            pltpu.VMEM((high, 128), f32),
            pltpu.SemaphoreType.DMA((rows,)),
            pltpu.SemaphoreType.DMA((3,)),
            pltpu.SemaphoreType.DMA((4,)),
            pltpu.SemaphoreType.DMA((4,)),
            pltpu.SemaphoreType.DMA((stages, rows, parts)),
            pltpu.SemaphoreType.DMA((stages, rows, parts)),
            pltpu.SemaphoreType.DMA((rows, parts)),
        ],
        compiler_params=pltpu.CompilerParams(
            collective_id=0, has_side_effects=True, vmem_limit_bytes=50 * 2**20),
        cost_estimate=pl.CostEstimate(
            flops=12 * high * high * rows * cols, bytes_accessed=8 * rows * high * cols,
            transcendentals=0),
    )(field, diffusivity, jnp.asarray(dft), jnp.asarray(shifts), jnp.asarray(factors))
    return result.reshape(rows, 2, count, cols).transpose(1, 2, 0, 3)


def solution(mesh):
    in_specs = (P(None, "tm", "space", None), P("space", None))
    out_specs = P(None, "tm", "space", None)
    return jax.shard_map(
        on_device, mesh=mesh, in_specs=in_specs, out_specs=out_specs, check_vma=False
    )
```

time: 501 us -> 235 us (0.47); the launches traced: 494 us -> 233 us
  Pallas kernels: 0 us -> 210 us
  waiting for transfers between devices: 119 us -> 0 us
  other arithmetic: 108 us -> 0 us
  blocking collectives: 95.7 us -> 0 us
  local copies, waits for them, and re-layouts: 110 us -> 23.4 us
  matrix products: 43 us -> 0 us
  starting transfers between devices: 16.3 us -> 0 us
    pallas_call x0 -> x1, Pallas kernels: none -> 210 us  [on_device(): pl.pallas_call(functools.partial(kernel, cfg), out_shape=jax.ShapeDtypeSt...]
    all_to_all x1 -> x0, blocking collectives: 95.7 us -> none  [on_device(): lax.all_to_all(outgoing, 'tm', split_axis=4, concat_axis=1, tiled=True)]
    all_to_all x1 -> x0, waiting for transfers between devices: 92.6 us -> none  [on_device(): lax.all_to_all(combined, 'tm', split_axis=1, concat_axis=4, tiled=True)]
    dot_general x5 -> x0, matrix products: 43 us -> none  [the longest x1 9.61 us: on_device(): jnp.dot(class_cos, arrived_real, precision=high)]
    unnamed x38 -> x8, local copies, waits for them, and re-layouts: 39.3 us -> 0.02 us
    sub x5 -> x0, other arithmetic: 38.4 us -> none  [the longest x2 18.7 us: on_device(): spectrum - applied]
    add x4 -> x0, other arithmetic: 31.3 us -> none  [the longest x2 22.5 us: apply_operator(): beside_all = from_north + from_south + from_west + from_east]
    ppermute x4 -> x0, waiting for transfers between devices: 26.6 us -> none  [the longest x2 17.8 us: extended_2(): lax.ppermute(lax.slice_in_dim(block, block.shape[dim] - width, None, axis...]
  transfers between devices with their start and end apart: 5 -> 0, of which waited for: 5 -> 0; matrix products, arithmetic and copies ran while one was open for 0% -> 0% of each run, Pallas kernels for 0% -> 0%
where the time goes in v1:
time: 235 us; the launch traced here: 233 us
  Pallas kernels  210 us (89%)
  local copies, waits for them, and re-layouts  23.4 us (10%)
    pallas_call x1, Pallas kernels, on_device(): pl.pallas_call(functools.partial(kernel, cfg), out_shape=jax.ShapeDtypeSt...  210 us
    transpose x1, local copies, waits for them, and re-layouts, on_device(): field = spectrum.transpose(2, 0, 1, 3).reshape(rows, 2 * count, cols)  11.8 us
    reshape x1, local copies, waits for them, and re-layouts, on_device(): return result.reshape(rows, 2, count, cols).transpose(1, 2, 0, 3)  11.6 us

profile of v1, /device:TPU:9, one launch (start us, length us, event | category | flops | bytes accessed | tf_op | source)
XLA Modules:
  0.0 233.2 jit_solution(10648245315661443683)
XLA Ops:
  0.0 0.0 copy-start
  0.0 0.0 copy-start.1
  0.0 0.0 copy-start.2
  0.0 0.0 copy-start.3
  0.0 11.8 %copy.6 = f32[8,2,128,1024]{3,2,1,0:T(8,128)} copy(f32[8,2,128,1024]{3,0,2,1:T(8,128)} %bitcast.6) | data formatting | bytes 16777216 | tf_op jit(solution)/shard_map/transpose | solution.py:367
  11.8 0.0 copy-done
  11.8 0.0 copy-done.1
  11.8 0.0 copy-done.2
  11.8 0.0 copy-done.3
  11.8 209.7 %shard_map.55 = f32[8,256,1024]{2,1,0:T(8,128)} custom-call(f32[8,256,1024]{2,1,0:T(8,128)} %bitcast.8, f32[8,1024]{1,0:T(8,128)S(1)} %copy-done, f32[4,256,256]{2,1,0:T(8,128)S(1)} %copy-done.1, f32[4,256,128]{2,1,0:T(8,128)S(1)} %copy-done.2, f32[32]{0:T(128)S(1)} %copy-done.3), custom_call_target="tpu_custom_call" | custom-call | flops 6442450944 | bytes 16777216 | tf_op jit(solution)/shard_map/pallas_call | solution.py:373
  221.5 11.6 %copy.9 = f32[8,2,128,1024]{3,0,2,1:T(8,128)} copy(f32[8,2,128,1024]{3,2,1,0:T(8,128)} %bitcast.7) | data formatting | bytes 16777216 | tf_op jit(solution)/shard_map/reshape | solution.py:400
Async XLA Ops:
  0.0 11.8 %copy-start = (f32[8,1024]{1,0:T(8,128)S(1)}, f32[8,1024]{1,0:T(8,128)}, u32[]{:S(2)}) copy-start(f32[8,1024]{1,0:T(8,128)} %diffusion.1) | copy-start | bytes 98308
  0.0 11.8 %copy-start.1 = (f32[4,256,256]{2,1,0:T(8,128)S(1)}, f32[4,256,256]{2,1,0:T(8,128)}, u32[]{:S(2)}) copy-start(f32[4,256,256]{2,1,0:T(8,128)} %constant.6.clone.dft_all) | copy-start | bytes 3145732
  0.0 11.8 %copy-start.2 = (f32[4,256,128]{2,1,0:T(8,128)S(1)}, f32[4,256,128]{2,1,0:T(8,128)}, u32[]{:S(2)}) copy-start(f32[4,256,128]{2,1,0:T(8,128)} %constant.7.clone.shift_all) | copy-start | bytes 1572868
  0.0 11.8 %copy-start.3 = (f32[32]{0:T(128)S(1)}, f32[32]{0:T(128)}, u32[]{:S(2)}) copy-start(f32[32]{0:T(128)} %constant.8.clone.factors) | copy-start | bytes 388

commit v2 on v1

--- a/solution.py
+++ b/solution.py
@@ -17,6 +17,7 @@
 ]
 MESH = pl.DeviceIdType.MESH
 HALO = 2
+GROUPS = 4
 
 
 def reverse_bits(number, bit_count):
@@ -59,7 +60,7 @@
 
 def kernel(
     cfg, field, diffusion, dft_all, shift_all, factors, out,
-    hold, mid, last, moved, grid_d, dft, shift,
+    raw, hold, mid, last, moved, grid_d, dft, shift,
     load_sem, table_sem, edge_send, edge_recv, move_send, move_recv, out_sem,
 ):
     stages, tm_count, count, rows, cols, parts, tile = cfg
@@ -84,10 +85,16 @@
         pl.semaphore_signal(barrier, inc=1, device_id={"space": s + 1}, device_id_type=MESH)
 
     row_order = [(turn + HALO) % rows for turn in range(rows)]
-    loads = {
-        row: pltpu.make_async_copy(field.at[row], hold.at[row + HALO], load_sem.at[row])
-        for row in range(rows)
-    }
+    group = count // GROUPS
+    loads = [
+        [
+            pltpu.make_async_copy(
+                field.at[pl.ds(half * count + part * group, group)],
+                raw.at[pl.ds(half * count + part * group, group)], load_sem.at[part, half])
+            for half in range(2)
+        ]
+        for part in range(GROUPS)
+    ]
     tables = [
         pltpu.make_async_copy(diffusion, grid_d.at[pl.ds(8, rows)], table_sem.at[0]),
         pltpu.make_async_copy(shift_all.at[d], shift, table_sem.at[1]),
@@ -95,13 +102,14 @@
     ]
     tables[0].start()
     tables[1].start()
-    for row in range(rows):
-        loads[row].start()
+    for pair in loads:
+        for copy in pair:
+            copy.start()
     tables[2].start()
 
     to_north = [
         pltpu.make_async_remote_copy(
-            field.at[pl.ds(0, HALO)], hold.at[pl.ds(rows + HALO, HALO)],
+            hold.at[pl.ds(HALO, HALO)], hold.at[pl.ds(rows + HALO, HALO)],
             edge_send.at[0], edge_recv.at[0], device_id={"space": s - 1}, device_id_type=MESH),
         pltpu.make_async_remote_copy(
             diffusion, grid_d.at[pl.ds(8 + rows, rows)],
@@ -109,26 +117,13 @@
     ]
     to_south = [
         pltpu.make_async_remote_copy(
-            field.at[pl.ds(rows - HALO, HALO)], hold.at[pl.ds(0, HALO)],
+            hold.at[pl.ds(rows, HALO)], hold.at[pl.ds(0, HALO)],
             edge_send.at[2], edge_recv.at[2], device_id={"space": s + 1}, device_id_type=MESH),
         pltpu.make_async_remote_copy(
             diffusion, grid_d.at[pl.ds(8 - rows, rows)],
             edge_send.at[3], edge_recv.at[3], device_id={"space": s + 1}, device_id_type=MESH),
     ]
 
-    beside = lax.div(s + s_count - 1, s_count) + lax.div(2 * (s_count - 1) - s, s_count)
-    pl.semaphore_wait(barrier, stages + beside)
-
-    @pl.when(not_first)
-    def _():
-        for copy in to_north:
-            copy.start()
-
-    @pl.when(not_last)
-    def _():
-        for copy in to_south:
-            copy.start()
-
     tables[0].wait()
     tables[1].wait()
 
@@ -142,11 +137,12 @@
 
         lax.fori_loop(0, count // 8, step, 0)
 
-    def inverse_diag(row, re, im):
+    def inverse_diag(row, re, im, cut=slice(None), span=None):
+        span = span or cols
         wide = jnp.concatenate
-        local = jnp.broadcast_to(grid_d[pl.ds(8 + row, 1), :], (8, cols))
-        diag_real = wide([shift[re, :]] * (cols // 128), axis=1) + (4.0 * local + flow_speed)
-        diag_imag = wide([shift[im, :]] * (cols // 128), axis=1)
+        local = jnp.broadcast_to(grid_d[pl.ds(8 + row, 1), cut], (8, span))
+        diag_real = wide([shift[re, :]] * (span // 128), axis=1) + (4.0 * local + flow_speed)
+        diag_imag = wide([shift[im, :]] * (span // 128), axis=1)
         scale = 1.0 / (diag_real * diag_real + diag_imag * diag_imag)
         return local, diag_real * scale, diag_imag * scale
 
@@ -163,16 +159,22 @@
 
     w0, w1, w2 = sweep_weights
 
-    def first_sweep(row):
-        at = row + HALO
-
-        def body(re, im):
-            _, g_real, g_imag = inverse_diag(row, re, im)
-            real, imag = over(hold[at, re, :], hold[at, im, :], g_real, g_imag)
-            hold[at, re, :] = w0 * real
-            hold[at, im, :] = w0 * imag
-
-        each_block(body)
+    def first_sweep(part):
+        def step(index, carry):
+            low = part * group + index // (cols // tile) * 8
+            cut = pl.ds(pl.multiple_of(index % (cols // tile) * tile, 128), tile)
+            re = pl.ds(pl.multiple_of(low, 8), 8)
+            im = pl.ds(pl.multiple_of(low + count, 8), 8)
+            real_rows = jnp.swapaxes(raw[re, :, cut], 0, 1)
+            imag_rows = jnp.swapaxes(raw[im, :, cut], 0, 1)
+            for row in range(rows):
+                _, g_real, g_imag = inverse_diag(row, re, im, cut, tile)
+                real, imag = over(real_rows[row], imag_rows[row], g_real, g_imag)
+                hold[row + HALO, re, cut] = w0 * real
+                hold[row + HALO, im, cut] = w0 * imag
+            return carry
+
+        lax.fori_loop(0, group // 8 * (cols // tile), step, 0)
 
     def second_sweep(row):
         at = row + HALO
@@ -241,71 +243,79 @@
         else:
             write_out(row, part).start()
 
-    done_first, done_second = set(), set()
+    for part in range(GROUPS):
+        for copy in loads[part]:
+            copy.wait()
+        first_sweep(part)
+
+    beside = lax.div(s + s_count - 1, s_count) + lax.div(2 * (s_count - 1) - s, s_count)
+    pl.semaphore_wait(barrier, stages + beside)
+
+    @pl.when(not_first)
+    def _():
+        for copy in to_north:
+            copy.start()
+
+    @pl.when(not_last)
+    def _():
+        for copy in to_south:
+            copy.start()
+
+    done = set()
 
     def north_edge():
         @pl.when(not_first)
         def _():
             for copy in to_south:
                 copy.wait_recv()
-            for row in range(-HALO, 0):
-                first_sweep(row)
+            second_sweep(-1)
 
         @pl.when(is_first)
         def _():
-            hold[1] = jnp.zeros((2 * count, cols), jnp.float32)
+            hold[HALO - 1] = jnp.zeros((2 * count, cols), jnp.float32)
             mid[0] = jnp.zeros((2 * count, cols), jnp.float32)
-
-        need_first(0)
-
-        @pl.when(not_first)
-        def _():
-            second_sweep(-1)
 
     def south_edge():
         @pl.when(not_last)
         def _():
             for copy in to_north:
                 copy.wait_recv()
-            for row in range(rows, rows + HALO):
-                first_sweep(row)
+            second_sweep(rows)
 
         @pl.when(is_last)
         def _():
             hold[rows + HALO] = jnp.zeros((2 * count, cols), jnp.float32)
             mid[rows + 1] = jnp.zeros((2 * count, cols), jnp.float32)
 
-        need_first(rows - 1)
-
-        @pl.when(not_last)
-        def _():
-            second_sweep(rows)
-
-    edges = {-1: north_edge, rows: south_edge}
-
-    def need_first(row):
-        if row in edges:
-            if edges[row] is not None:
-                run, edges[row] = edges[row], None
-                run()
-        elif row not in done_first:
-            done_first.add(row)
-            loads[row].wait()
-            first_sweep(row)
-
     def need_second(row):
-        if row in edges:
-            need_first(row)
-        elif row not in done_second:
-            done_second.add(row)
-            for near in (row - 1, row, row + 1):
-                need_first(near)
+        if row in done:
+            return
+        done.add(row)
+        if row == -1:
+            north_edge()
+        elif row == rows:
+            south_edge()
+        else:
+            if row == 0:
+                need_second(-1)
+            if row == rows - 1:
+                need_second(rows)
             second_sweep(row)
 
     def solve_row(row, first):
         for near in (row - 1, row, row + 1):
             need_second(near)
         third_sweep(row)
+        if row == 0:
+            @pl.when(not_first)
+            def _():
+                to_north[0].wait_send()
+
+        if row == rows - HALO:
+            @pl.when(not_last)
+            def _():
+                to_south[0].wait_send()
+
         if first:
             tables[2].wait()
         for part in range(parts):
@@ -350,21 +360,36 @@
 
     @pl.when(not_first)
     def _():
-        for copy in to_north:
-            copy.wait_send()
+        to_north[1].wait_send()
 
     @pl.when(not_last)
     def _():
-        for copy in to_south:
-            copy.wait_send()
+        to_south[1].wait_send()
+
+
+def swap_kernel(source, target):
+    target[...] = jnp.swapaxes(source[...], 0, 1)
+
+
+def swap_rows(field):
+    rows, high, cols = field.shape
+    block = 32
+    return pl.pallas_call(
+        swap_kernel,
+        grid=(high // block,),
+        out_shape=jax.ShapeDtypeStruct((high, rows, cols), field.dtype),
+        in_specs=[pl.BlockSpec((rows, block, cols), lambda i: (0, i, 0))],
+        out_specs=pl.BlockSpec((block, rows, cols), lambda i: (i, 0, 0)),
+        compiler_params=pltpu.CompilerParams(vmem_limit_bytes=60 * 2**20),
+    )(field)
 
 
 def on_device(spectrum, diffusivity):
     count, rows, cols = spectrum.shape[1:]
     tm_count = lax.axis_size("tm")
     stages = tm_count.bit_length() - 1
-    parts, tile = 2, 256
-    field = spectrum.transpose(2, 0, 1, 3).reshape(rows, 2 * count, cols)
+    parts, tile = 4, 256
+    field = spectrum.reshape(2 * count, rows, cols)
     dft, shifts, factors = make_tables(tm_count, count)
     cfg = (stages, tm_count, count, rows, cols, parts, tile)
     high = 2 * count
@@ -376,6 +401,7 @@
         in_specs=[anywhere] * 4 + [pl.BlockSpec(memory_space=pltpu.SMEM)],
         out_specs=anywhere,
         scratch_shapes=[
+            pltpu.VMEM((high, rows, cols), f32),
             pltpu.VMEM((rows + 2 * HALO, high, cols), f32),
             pltpu.VMEM((rows + 2, high, cols), f32),
             pltpu.VMEM((high, cols), f32),
@@ -383,7 +409,7 @@
             pltpu.VMEM((8 + 2 * rows, cols), f32),
             pltpu.VMEM((high, high), f32),
             pltpu.VMEM((high, 128), f32),
-            pltpu.SemaphoreType.DMA((rows,)),
+            pltpu.SemaphoreType.DMA((GROUPS, 2)),
             pltpu.SemaphoreType.DMA((3,)),
             pltpu.SemaphoreType.DMA((4,)),
             pltpu.SemaphoreType.DMA((4,)),
@@ -392,12 +418,12 @@
             pltpu.SemaphoreType.DMA((rows, parts)),
         ],
         compiler_params=pltpu.CompilerParams(
-            collective_id=0, has_side_effects=True, vmem_limit_bytes=50 * 2**20),
+            collective_id=0, has_side_effects=True, vmem_limit_bytes=56 * 2**20),
         cost_estimate=pl.CostEstimate(
             flops=12 * high * high * rows * cols, bytes_accessed=8 * rows * high * cols,
             transcendentals=0),
     )(field, diffusivity, jnp.asarray(dft), jnp.asarray(shifts), jnp.asarray(factors))
-    return result.reshape(rows, 2, count, cols).transpose(1, 2, 0, 3)
+    return swap_rows(result).reshape(2, count, rows, cols)
 
 
 def solution(mesh):

time: 235 us -> 224 us (0.953)
  local copies, waits for them, and re-layouts: 23.4 us -> 0 us
  Pallas kernels: 210 us -> 222 us
    transpose x1 -> x0, local copies, waits for them, and re-layouts: 11.8 us -> none  [on_device(): field = spectrum.transpose(2, 0, 1, 3).reshape(rows, 2 * count, cols)]
    reshape x1 -> x0, local copies, waits for them, and re-layouts: 11.6 us -> none  [on_device(): return result.reshape(rows, 2, count, cols).transpose(1, 2, 0, 3)]
    pallas_call x0 -> x1, Pallas kernels: none -> 9.42 us  [swap_rows(): pl.pallas_call(swap_kernel, grid=(high // block,), out_shape=jax.ShapeDty...]
    pallas_call x1, Pallas kernels: 210 us -> 212 us  [on_device(): pl.pallas_call(functools.partial(kernel, cfg), out_shape=jax.ShapeDtypeSt...]
where the time goes in v2:
time: 224 us; the launch traced here: 222 us
  Pallas kernels  222 us (99%)
    pallas_call x1, Pallas kernels, on_device(): pl.pallas_call(functools.partial(kernel, cfg), out_shape=jax.ShapeDtypeSt...  212 us
    pallas_call x1, Pallas kernels, swap_rows(): pl.pallas_call(swap_kernel, grid=(high // block,), out_shape=jax.ShapeDty...  9.42 us

profile of v2, /device:TPU:9, one launch (start us, length us, event | category | flops | bytes accessed | tf_op | source)
XLA Modules:
  0.0 221.8 jit_solution(16575264972935433949)
XLA Ops:
  0.0 212.4 %shard_map.55.source = f32[8,256,1024]{2,1,0:T(8,128)} custom-call(f32[256,8,1024]{2,1,0:T(8,128)} %bitcast.2, f32[8,1024]{1,0:T(8,128)} %diffusion.1, f32[4,256,256]{2,1,0:T(8,128)} %constant.6.clone.dft_all, f32[4,256,128]{2,1,0:T(8,128)} %constant.7.clone.shift_all, f32[32]{0:T(128)} %constant.8.clone.factors), custom_call_target="tpu_custom_call" | custom-call | flops 6442450944 | bytes 16777216 | tf_op jit(solution)/shard_map/pallas_call | solution.py:398
  212.4 9.4 %shard_map.56 = f32[256,8,1024]{2,1,0:T(8,128)} custom-call(f32[8,256,1024]{2,1,0:T(8,128)} %shard_map.55.source), custom_call_target="tpu_custom_call" | custom-call | tf_op jit(solution)/shard_map/pallas_call | solution.py:377

commit v3 on v2

--- a/solution.py
+++ b/solution.py
@@ -143,8 +143,17 @@
         local = jnp.broadcast_to(grid_d[pl.ds(8 + row, 1), cut], (8, span))
         diag_real = wide([shift[re, :]] * (span // 128), axis=1) + (4.0 * local + flow_speed)
         diag_imag = wide([shift[im, :]] * (span // 128), axis=1)
-        scale = 1.0 / (diag_real * diag_real + diag_imag * diag_imag)
+        magnitude = diag_real * diag_real + diag_imag * diag_imag
+        guess = pl.reciprocal(magnitude, approx=True)
+        guess = guess * (2.0 - magnitude * guess)
+        scale = guess * (2.0 - magnitude * guess)
         return local, diag_real * scale, diag_imag * scale
+
+    def kept_inverse(row, re, im):
+        if not 0 <= row < rows:
+            return inverse_diag(row, re, im)
+        local = jnp.broadcast_to(grid_d[pl.ds(8 + row, 1), :], (8, cols))
+        return local, raw[re.start + row], raw[im.start + row]
 
     def over(real, imag, g_real, g_imag):
         return real * g_real + imag * g_imag, imag * g_real - real * g_imag
@@ -172,6 +181,8 @@
                 real, imag = over(real_rows[row], imag_rows[row], g_real, g_imag)
                 hold[row + HALO, re, cut] = w0 * real
                 hold[row + HALO, im, cut] = w0 * imag
+                raw[low + row, :, cut] = g_real
+                raw[low + count + row, :, cut] = g_imag
             return carry
 
         lax.fori_loop(0, group // 8 * (cols // tile), step, 0)
@@ -181,7 +192,7 @@
         keep = 1.0 - w1 + w1 / w0
 
         def body(re, im):
-            local, g_real, g_imag = inverse_diag(row, re, im)
+            local, g_real, g_imag = kept_inverse(row, re, im)
             here_real, pull_real = pull(hold, at, re, local)
             here_imag, pull_imag = pull(hold, at, im, local)
             real, imag = over(pull_real, pull_imag, g_real, g_imag)
@@ -192,7 +203,7 @@
 
     def third_sweep(row):
         def body(re, im):
-            local, g_real, g_imag = inverse_diag(row, re, im)
+            local, g_real, g_imag = kept_inverse(row, re, im)
             here_real, pull_real = pull(mid, row + 1, re, local)
             here_imag, pull_imag = pull(mid, row + 1, im, local)
             real, imag = over(pull_real, pull_imag, g_real, g_imag)
@@ -330,25 +341,27 @@
             exchange(0, row, part).start()
 
     chunks = rows * parts
-    lags = [1 + 2 * stage for stage in range(stages)]
-    uniform = range(max(rows, lags[-1]), chunks + 1)
+    lags = [2 * stage for stage in range(stages)]
+    pace = 2
 
     def tick(now, checked):
         for stage in range(stages):
             if not checked or 0 <= now - lags[stage] < chunks:
                 combine(stage, now - lags[stage])
 
-    for now in range(uniform.start):
-        if now < rows:
-            solve_row(row_order[now], now == 0)
-        tick(now, True)
+    solve_row(row_order[0], True)
+    for turn in range(1, rows):
+        solve_row(row_order[turn], False)
+        for now in range(pace * (turn - 1), pace * turn):
+            tick(now, True)
+    begin = pace * (rows - 1)
 
     def steady(now, carry):
         tick(now, False)
         return carry
 
-    lax.fori_loop(uniform.start, uniform.stop, steady, 0)
-    for now in range(uniform.stop, chunks + lags[-1]):
+    lax.fori_loop(begin, chunks, steady, 0)
+    for now in range(chunks, chunks + lags[-1]):
         tick(now, True)
 
     def finish(chunk, carry):

time: 224 us -> 223 us (level)
  Pallas kernels: 222 us -> 219 us
    pallas_call x1, Pallas kernels: 212 us -> 210 us  [on_device(): pl.pallas_call(functools.partial(kernel, cfg), out_shape=jax.ShapeDtypeSt...]
where the time goes in v3:
time: 223 us; the launch traced here: 219 us
  Pallas kernels  219 us (98%)
    pallas_call x1, Pallas kernels, on_device(): pl.pallas_call(functools.partial(kernel, cfg), out_shape=jax.ShapeDtypeSt...  210 us
    pallas_call x1, Pallas kernels, swap_rows(): pl.pallas_call(swap_kernel, grid=(high // block,), out_shape=jax.ShapeDty...  9.42 us

profile of v3, /device:TPU:9, one launch (start us, length us, event | category | flops | bytes accessed | tf_op | source)
XLA Modules:
  0.0 219.1 jit_solution(1087831990915693921)
XLA Ops:
  0.0 209.6 %shard_map.55.source = f32[8,256,1024]{2,1,0:T(8,128)} custom-call(f32[256,8,1024]{2,1,0:T(8,128)} %bitcast.2, f32[8,1024]{1,0:T(8,128)} %diffusion.1, f32[4,256,256]{2,1,0:T(8,128)} %constant.6.clone.dft_all, f32[4,256,128]{2,1,0:T(8,128)} %constant.7.clone.shift_all, f32[32]{0:T(128)} %constant.8.clone.factors), custom_call_target="tpu_custom_call" | custom-call | flops 6442450944 | bytes 16777216 | tf_op jit(solution)/shard_map/pallas_call | solution.py:411
  209.7 9.4 %shard_map.56 = f32[256,8,1024]{2,1,0:T(8,128)} custom-call(f32[8,256,1024]{2,1,0:T(8,128)} %shard_map.55.source), custom_call_target="tpu_custom_call" | custom-call | tf_op jit(solution)/shard_map/pallas_call | solution.py:390
